TPU v7x, 32 devices: a whole 2x2x4 slice. The times are simulated.
32 devices in a mesh: gx: 4 (over x, core), gy: 4 (over z), gz: 2 (over y).
Axes of the slice: x: 2, y: 2, z: 4, core: 2. Of those that a mesh axis runs over, the one named last changes fastest.
Arguments:
- field: float32 [2, 32, 256, 512], P(None, 'gz', 'gx', 'gy'), may hold values from -30 to 30
- transfer: float32 [4, 128], replicated, may hold values from 0.2 to 3
- light_angles: float32 [2], replicated, may hold values from -3.140625 to 3.140625
Outputs:
- image: float32 [4, 256, 512], P(None, ('gx', 'gz'), 'gy')
All inputs are finite; a program needn't handle non-finite values.
Results may differ from a plain program's by a relative error of at most 0.00019.
Values sent between devices are 32-bit elements; how exact they have to be, the bound alone decides.
A program may use at most 64 MiB of HBM per device.

v0:
```python
import functools
import math

import jax
import jax.numpy as jnp
from jax import lax
from jax.experimental import pallas as pl
from jax.experimental.pallas import tpu as pltpu
from jax.sharding import PartitionSpec as P

MESH = pl.DeviceIdType.MESH
SIGMA_TAPS = 1.2
OPTICAL = 2.0
SHADE_FLOOR = 0.25
EDGE = 8


def filter_taps():
    places = [-3, -2, -1, 0, 1, 2, 3]
    bell = [math.exp(-place * place / (2.0 * SIGMA_TAPS * SIGMA_TAPS)) for place in places]
    bell_total = sum(bell)
    slope_total = sum((place * place * weight for place, weight in zip(places, bell)))
    smooth_taps = [weight / bell_total for weight in bell]
    slope_taps = [place * weight / slope_total for place, weight in zip(places, bell)]
    return (smooth_taps, slope_taps)


def smooth_of(at):
    taps, _ = filter_taps()
    total = taps[3] * at(0)
    for o in (1, 2, 3):
        total = total + taps[3 + o] * (at(o) + at(-o))
    return total


def slope_of(at):
    _, taps = filter_taps()
    total = taps[4] * (at(1) - at(-1))
    for o in (2, 3):
        total = total + taps[3 + o] * (at(o) - at(-o))
    return total


def both_of(at):
    smooth, slope = filter_taps()
    plain, steep = smooth[3] * at(0), None
    for o in (1, 2, 3):
        after, before = at(o), at(-o)
        plain = plain + smooth[3 + o] * (after + before)
        term = slope[3 + o] * (after - before)
        steep = term if steep is None else steep + term
    return plain, steep


def kernel(sizes, depth_step, field, transfer_in, angles_in, out, transfer, angles, box, own_strips, rim_strips, got_own, got_rim, joined,
           rows_done, flat_done, table, light, inner, stage, slabs,
           local_sem, small_sem, send_sem, recv_sem, slab_send, slab_recv):
    nx, ny, nz = sizes
    _, depth, rows, lanes = field.shape
    total = rows + 2 * EDGE
    ix, iy, iz = (lax.axis_index(name) for name in ("gx", "gy", "gz"))
    spots = (("gx", ix, nx), ("gy", iy, ny), ("gz", iz, nz))

    def has(way):
        need = None
        for (_, place, count), step in zip(spots, way):
            if step:
                here = place > 0 if step < 0 else place < count - 1
                need = here if need is None else jnp.logical_and(need, here)
        return need

    def target(way):
        return {name: place + step for (name, place, _), step in zip(spots, way) if step}

    def lies(axis, step):
        return tuple(step if k == axis else 0 for k in range(3))

    flat_ways = [(dx, dy, 0) for dx in (-1, 0, 1) for dy in (-1, 0, 1) if dx or dy]
    sides = (-1, 1)

    barrier = pltpu.get_barrier_semaphore()
    for way in flat_ways:
        @pl.when(has(way))
        def _():
            pl.semaphore_signal(barrier, inc=1, device_id=target(way), device_id_type=MESH)
    for j in range(1, nz):
        pl.semaphore_signal(barrier, inc=1, device_id={"gz": lax.rem(iz + j, nz)}, device_id_type=MESH)

    own = pltpu.make_async_copy(
        field, box.at[:, pl.ds(3, depth), pl.ds(EDGE, rows), :], local_sem)
    own.start()
    small = (pltpu.make_async_copy(transfer_in, transfer, small_sem.at[0]),
             pltpu.make_async_copy(angles_in, angles, small_sem.at[1]))
    for each in small:
        each.start()

    for step in sides:
        edge = 0 if step < 0 else EDGE + rows
        @pl.when(jnp.logical_not(has(lies(0, step))))
        def _():
            box[:, :, edge:edge + EDGE, :] = jnp.zeros((2, depth + 6, EDGE, lanes), jnp.float32)
            got_own[:, :, edge:edge + EDGE, :] = jnp.zeros((2, 2, EDGE, lanes), jnp.float32)
        first = 0 if step < 0 else depth + 3
        @pl.when(jnp.logical_not(has(lies(2, step))))
        def _():
            flat_done[:, first:first + 3] = jnp.zeros((4, 3, rows, lanes), jnp.float32)
        side = 0 if step < 0 else 1
        @pl.when(jnp.logical_not(has(lies(1, step))))
        def _():
            got_own[side] = jnp.zeros((2, total, lanes), jnp.float32)

    links = {}

    def link(name, way, src, dst, need=None):
        links[name, way] = (len(links), src, dst, need)

    def wanted(name, way):
        need, more = has(way), links[name, way][3]
        return need if more is None else jnp.logical_and(need, more)

    def copy(name, way):
        slot, src, dst, _ = links[name, way]
        return pltpu.make_async_remote_copy(
            src_ref=src, dst_ref=dst, send_sem=send_sem.at[slot], recv_sem=recv_sem.at[slot],
            device_id=target(way), device_id_type=MESH)

    def begin(name, way):
        @pl.when(wanted(name, way))
        def _():
            copy(name, way).start()

    def sent(name, way):
        @pl.when(wanted(name, way))
        def _():
            copy(name, way).wait_send()

    def got(name, way):
        back = tuple(-step for step in way)
        need, more = has(way), links[name, back][3]
        @pl.when(need if more is None else jnp.logical_and(need, more))
        def _():
            copy(name, back).wait_recv()

    every = pl.ds(3, depth)
    middle = pl.ds(EDGE, rows)

    def rows_from(dx):
        return middle if dx == 0 else pl.ds(EDGE if dx < 0 else rows, EDGE)

    def rows_to(dx):
        return middle if dx == 0 else pl.ds(EDGE + rows if dx < 0 else 0, EDGE)

    for way in flat_ways:
        if way[1]:
            side = 0 if way[1] > 0 else 1
            link("strips", way, own_strips.at[:, rows_from(way[0]), :], got_own.at[side, :, rows_to(way[0]), :])
    for step in sides:
        row = 0 if step < 0 else rows - EDGE
        link("rows", lies(0, step), field.at[:, :, pl.ds(row, EDGE), :], box.at[:, every, rows_to(step), :])
        plane = 0 if step < 0 else depth - 3
        to = depth + 3 if step < 0 else 0
        link("planes", lies(2, step), field.at[:, pl.ds(plane, 3)], box.at[:, pl.ds(to, 3), middle, :])
        for name, at, side in (("low", 0, -1), ("high", EDGE + rows, 1)):
            link(name, lies(2, step), box.at[:, pl.ds(3 + plane, 3), pl.ds(at, EDGE), :],
                 box.at[:, pl.ds(to, 3), pl.ds(at, EDGE), :], has(lies(0, side)))
        link("rims", lies(2, step), rim_strips.at[0 if step < 0 else 1], got_rim.at[0 if step > 0 else 1])

    count = nz - 1
    for way in flat_ways:
        count = count + has(way).astype(jnp.int32)

    lane = lax.broadcasted_iota(jnp.int32, (total, lanes), 1)

    def in_group(lane, group):
        return jnp.bitwise_and(lane + (3 + lanes) - 8 * group, lanes - 1) < 6

    pl.semaphore_wait(barrier, count)
    for step in sides:
        begin("planes", lies(2, step))
    for step in sides:
        begin("rows", lies(0, step))
    own.wait()
    group_count = 4 if depth % 4 == 0 else 1

    def pack(i, kept):
        for p in range(group_count):
            z = i * group_count + p
            mask = in_group(lane[:rows], z)
            kept = tuple(
                jnp.where(mask, pltpu.roll(box[v, 3 + z, EDGE:EDGE + rows, :], 8 * z, 1), kept[v])
                for v in range(2))
        return kept

    empty = jnp.zeros((rows, lanes), jnp.float32)
    packed = lax.fori_loop(0, depth // group_count, pack, (empty, empty))
    for v in range(2):
        own_strips[v, EDGE:EDGE + rows, :] = packed[v]

    strip_ways = [way for way in flat_ways if way[1]]
    for way in strip_ways:
        begin("strips", way)

    for each in small:
        each.wait()
    azimuth = jnp.full(light.shape[1:], angles[0], jnp.float32)
    polar = jnp.full(light.shape[1:], angles[1], jnp.float32)
    light[0] = jnp.cos(azimuth) * jnp.sin(polar)
    light[1] = jnp.sin(azimuth) * jnp.sin(polar)
    light[2] = jnp.cos(polar)
    for c in range(4):
        line = jnp.broadcast_to(transfer[c:c + 1, :], table.shape[1:])
        table[2 * c] = line
        table[2 * c + 1] = pltpu.roll(line, lanes - 1, 1) - line

    def merged(left, right):
        here = jnp.bitwise_and(lax.broadcasted_iota(jnp.int32, left.shape, 1), 7)
        return jnp.where(here >= 4, left, right)

    def along_y(v, plane, at, count, group, strips):
        here = lane[:count]
        block = box[v, plane, at:at + count, :]
        halo = pltpu.roll(strips, lanes - 8 * group, 1)

        def place(o):
            if o == 0:
                return block
            if o > 0:
                return pltpu.roll(jnp.where(here < o, halo, block), lanes - o, 1)
            return pltpu.roll(jnp.where(here >= lanes + o, halo, block), -o, 1)

        return both_of(place) if v == 0 else (smooth_of(place),)

    def own_y(blocks, planes):
        def turn(i, carry):
            done = []
            for p in range(planes):
                z = i * planes + p
                for at, count in blocks:
                    found = []
                    for v in range(2):
                        found += along_y(v, z + 3, at, count, z, joined[v, at:at + count, :])
                    done.append((z + 3, at, count, found))
            for plane, at, count, found in done:
                for k in range(3):
                    rows_done[k, plane, at:at + count, :] = found[k]
            return carry
        lax.fori_loop(0, depth // planes, turn, 0)

    def along_x(plane):
        width = 32 if rows % 32 == 0 else EDGE
        for at in range(0, rows, width):
            def reader(k):
                return lambda o: rows_done[k, plane, EDGE + at + o:EDGE + at + o + width, :]
            plain, steep = both_of(reader(0))
            crossed, other = smooth_of(reader(1)), smooth_of(reader(2))
            for k, found in enumerate((plain, steep, crossed, other)):
                flat_done[k, plane, at:at + width, :] = found

    def own_x(z, carry):
        along_x(z + 3)
        return carry

    for step, name in ((-1, "low"), (1, "high")):
        got("rows", lies(0, step))
        for side in sides:
            begin(name, lies(2, side))
    for way in strip_ways:
        got("strips", way)
    for v in range(2):
        joined[v] = merged(got_own[0, v], got_own[1, v])
    for step in sides:
        plane = 0 if step < 0 else depth - 3
        second = jnp.logical_and(lane >= 40, lane < 104)
        rim_strips[0 if step < 0 else 1] = jnp.where(
            second, pltpu.roll(joined[1], (8 * (8 - plane)) % lanes, 1),
            pltpu.roll(joined[0], (8 * (lanes // 8 - plane)) % lanes, 1))
        begin("rims", lies(2, step))
    own_y([(at, 40) for at in range(0, total, 40)], 1)
    lax.fori_loop(0, depth, own_x, 0)

    rims = {-1: ((0, 0), (1, 1), (2, 2)), 1: tuple((h, depth + 3 + h) for h in range(3))}

    def sample(z, at, chunk):
        def reader(k):
            return lambda o: flat_done[k, z + 3 + o, pl.ds(at, chunk), :]
        value, grad_z = both_of(reader(0))
        grad_x = smooth_of(reader(1))
        grad_y = smooth_of(reader(2))
        mixture = smooth_of(reader(3))
        position = 0.5 * (lanes - 1) + (0.5 * (lanes - 1)) * jnp.tanh(0.5 * value)
        index = jnp.minimum(position.astype(jnp.int32), lanes - 2)
        share = position - index.astype(jnp.float32)

        def look(c):
            low = jnp.take_along_axis(table[2 * c, :chunk], index, axis=1, mode="promise_in_bounds")
            rise = jnp.take_along_axis(table[2 * c + 1, :chunk], index, axis=1, mode="promise_in_bounds")
            return low + share * rise

        facing = grad_x * light[0, :chunk] + grad_y * light[1, :chunk] + grad_z * light[2, :chunk]
        square = grad_x * grad_x + grad_y * grad_y + grad_z * grad_z + SHADE_FLOOR
        shade = 0.25 + 0.75 * (facing * facing / square)
        alpha = 1.0 - jnp.exp((-0.5 * OPTICAL * depth_step) * look(3) * (1.0 + jnp.tanh(0.5 * mixture)))
        lit = alpha * shade
        return (lit * look(0), lit * look(1), lit * look(2), alpha)

    def over(front, back):
        left = 1.0 - front[3]
        return tuple(f + left * b for f, b in zip(front, back))

    def nothing(chunk):
        return tuple(jnp.zeros((chunk, lanes), jnp.float32) for _ in range(4))

    wide = light.shape[1]

    height = rows // nz
    inner_rows = min(height, wide)

    def inner_slab(slab):
        def inner_chunk(c, carry):
            at = pl.multiple_of(slab * height + c * inner_rows, inner_rows)

            def turn(i, acc):
                z = 3 + 2 * i
                pair = [sample(z + p, at, inner_rows) for p in range(2)]
                return over(acc, over(*pair))

            result = lax.fori_loop(0, (depth - 6) // 2, turn, nothing(inner_rows))
            for k in range(4):
                inner[k, pl.ds(at, inner_rows), :] = result[k]
            return carry

        lax.fori_loop(0, height // inner_rows, inner_chunk, 0)

    for j in range(1, nz):
        inner_slab(lax.rem(iz + j, nz))

    for step in sides:
        for name in ("planes", "low", "high", "rims"):
            got(name, lies(2, step))

    for step in sides:
        @pl.when(has(lies(2, step)))
        def _():
            for h, plane in rims[step]:
                for at in range(0, total, 40):
                    found = []
                    for v in range(2):
                        found += along_y(v, plane, at, 40, 8 * v + h, got_rim[0 if step < 0 else 1, at:at + 40, :])
                    for k in range(3):
                        rows_done[k, plane, at:at + 40, :] = found[k]
            for h, plane in rims[step]:
                along_x(plane)

    def slab_copy(j):
        return pltpu.make_async_remote_copy(
            src_ref=stage.at[j - 1], dst_ref=slabs.at[iz], send_sem=slab_send.at[j - 1],
            recv_sem=slab_recv.at[iz], device_id={"gz": lax.rem(iz + j, nz)}, device_id_type=MESH)

    for j in range(1, nz + 1):
        slab = lax.rem(iz + j, nz)
        if j == nz:
            inner_slab(slab)

        at = pl.multiple_of(slab * height, height)
        acc = sample(0, at, height)
        for z in (1, 2):
            acc = over(acc, sample(z, at, height))
        acc = over(acc, tuple(inner[k, pl.ds(at, height), :] for k in range(4)))
        for z in range(depth - 3, depth):
            acc = over(acc, sample(z, at, height))
        for k in range(4):
            if j < nz:
                stage[j - 1, k] = acc[k]
            else:
                slabs[iz, k] = acc[k]
        if j < nz:
            slab_copy(j).start()

    for j in range(1, nz):
        source = lax.rem(iz + j, nz)
        pltpu.make_async_remote_copy(
            src_ref=stage.at[j - 1], dst_ref=slabs.at[source], send_sem=slab_send.at[j - 1],
            recv_sem=slab_recv.at[source], device_id={"gz": source}, device_id_type=MESH).wait_recv()

    image = tuple(slabs[0, k] for k in range(4))
    for k in range(1, nz):
        image = over(image, tuple(slabs[k, c] for c in range(4)))
    for c in range(4):
        out[c] = image[c]

    for name, way in links:
        sent(name, way)
    for j in range(1, nz):
        slab_copy(j).wait_send()


def shards(sizes, field, transfer, light_angles):
    nx, ny, nz = sizes
    _, depth, rows, lanes = field.shape
    total = rows + 2 * EDGE
    height = rows // nz
    chunk = 32
    full = depth + 6
    f32 = jnp.float32
    return pl.pallas_call(
        functools.partial(kernel, sizes, 1.0 / (depth * nz)),
        out_shape=jax.ShapeDtypeStruct((4, height, lanes), f32),
        in_specs=[
            pl.BlockSpec(memory_space=pltpu.HBM),
            pl.BlockSpec(memory_space=pltpu.HBM),
            pl.BlockSpec(memory_space=pltpu.HBM),
        ],
        out_specs=pl.BlockSpec(memory_space=pltpu.VMEM),
        scratch_shapes=[
            pltpu.VMEM((4, lanes), f32),
            pltpu.SMEM((2,), f32),
            pltpu.VMEM((2, full, total, lanes), f32),
            pltpu.VMEM((2, total, lanes), f32),
            pltpu.VMEM((2, total, lanes), f32),
            pltpu.VMEM((2, 2, total, lanes), f32),
            pltpu.VMEM((2, total, lanes), f32),
            pltpu.VMEM((2, total, lanes), f32),
            pltpu.VMEM((3, full, total, lanes), f32),
            pltpu.VMEM((4, full, rows, lanes), f32),
            pltpu.VMEM((8, chunk, lanes), f32),
            pltpu.VMEM((3, chunk, lanes), f32),
            pltpu.VMEM((4, rows, lanes), f32),
            pltpu.VMEM((nz - 1, 4, height, lanes), f32),
            pltpu.VMEM((nz, 4, height, lanes), f32),
            pltpu.SemaphoreType.DMA,
            pltpu.SemaphoreType.DMA((2,)),
            pltpu.SemaphoreType.DMA((20,)),
            pltpu.SemaphoreType.DMA((20,)),
            pltpu.SemaphoreType.DMA((nz,)),
            pltpu.SemaphoreType.DMA((nz,)),
        ],
        compiler_params=pltpu.CompilerParams(
            collective_id=0, has_side_effects=True, vmem_limit_bytes=40 * 1024 * 1024),
    )(*(pltpu.with_memory_space_constraint(x, pltpu.HBM) for x in (field, transfer, light_angles)))


def solution(mesh):
    sizes = tuple(mesh.shape[name] for name in ("gx", "gy", "gz"))
    placed = (P(None, "gz", "gx", "gy"), P(), P())
    return jax.shard_map(
        functools.partial(shards, sizes), mesh=mesh, in_specs=placed,
        out_specs=P(None, ("gx", "gz"), "gy"), check_vma=False
    )
```

profile of v0, /device:TPU:0, one launch (start us, length us, event | category | flops | bytes accessed | tf_op | source)
XLA Modules:
  0.0 22.7 jit_solution(11163048859266033489)
XLA Ops:
  0.0 22.1 %shard_map.37 = f32[4,32,128]{2,1,0:T(8,128)S(1)} custom-call(f32[2,16,64,128]{3,2,1,0:T(8,128)} %field.1, f32[4,128]{1,0:T(4,128)} %transfer_in.1, f32[2]{0:T(128)} %angles_in.1), custom_call_target="tpu_custom_call" | custom-call | tf_op jit(solution)/shard_map/pallas_call | solution.py:405
  22.1 0.6 %copy.5 = f32[4,32,128]{2,1,0:T(8,128)} copy(f32[4,32,128]{2,1,0:T(8,128)S(1)} %shard_map.37) | data formatting | bytes 131072
where the time goes:
time: 22.9 us; the launch traced here: 22.7 us
  Pallas kernels  22.1 us (97%)
  local copies, waits for them, and re-layouts  0.63 us (3%)
    pallas_call x1, Pallas kernels, shards(): pl.pallas_call(functools.partial(kernel, sizes, 1.0 / (depth * nz)), out_...  22.1 us
    unnamed x1, local copies, waits for them, and re-layouts  0.63 us

commit v1 on v0

--- a/solution.py
+++ b/solution.py
@@ -275,7 +275,7 @@
             second, pltpu.roll(joined[1], (8 * (8 - plane)) % lanes, 1),
             pltpu.roll(joined[0], (8 * (lanes // 8 - plane)) % lanes, 1))
         begin("rims", lies(2, step))
-    own_y([(at, 40) for at in range(0, total, 40)], 1)
+    own_y([(at, 40) for at in range(0, total, 40)], 2 if depth % 2 == 0 else 1)
     lax.fori_loop(0, depth, own_x, 0)
 
     rims = {-1: ((0, 0), (1, 1), (2, 2)), 1: tuple((h, depth + 3 + h) for h in range(3))}
@@ -315,16 +315,18 @@
     height = rows // nz
     inner_rows = min(height, wide)
 
+    run = next(k for k in (5, 2, 1) if (depth - 6) % k == 0)
+
     def inner_slab(slab):
         def inner_chunk(c, carry):
             at = pl.multiple_of(slab * height + c * inner_rows, inner_rows)
 
             def turn(i, acc):
-                z = 3 + 2 * i
-                pair = [sample(z + p, at, inner_rows) for p in range(2)]
-                return over(acc, over(*pair))
-
-            result = lax.fori_loop(0, (depth - 6) // 2, turn, nothing(inner_rows))
+                for p in range(run):
+                    acc = over(acc, sample(3 + run * i + p, at, inner_rows))
+                return acc
+
+            result = lax.fori_loop(0, (depth - 6) // run, turn, nothing(inner_rows))
             for k in range(4):
                 inner[k, pl.ds(at, inner_rows), :] = result[k]
             return carry

time: 22.9 us -> 23.1 us (level)
  no operation moved by 1% of the time
where the time goes in v1:
time: 23.1 us; the launch traced here: 23 us
  Pallas kernels  22.3 us (97%)
  local copies, waits for them, and re-layouts  0.63 us (3%)
    pallas_call x1, Pallas kernels, shards(): pl.pallas_call(functools.partial(kernel, sizes, 1.0 / (depth * nz)), out_...  22.3 us
    unnamed x1, local copies, waits for them, and re-layouts  0.63 us

profile of v1, /device:TPU:0, one launch (start us, length us, event | category | flops | bytes accessed | tf_op | source)
XLA Modules:
  0.0 23.0 jit_solution(471152520250617549)
XLA Ops:
  0.0 22.3 %shard_map.37 = f32[4,32,128]{2,1,0:T(8,128)S(1)} custom-call(f32[2,16,64,128]{3,2,1,0:T(8,128)} %field.1, f32[4,128]{1,0:T(4,128)} %transfer_in.1, f32[2]{0:T(128)} %angles_in.1), custom_call_target="tpu_custom_call" | custom-call | tf_op jit(solution)/shard_map/pallas_call | solution.py:407
  22.3 0.6 %copy.5 = f32[4,32,128]{2,1,0:T(8,128)} copy(f32[4,32,128]{2,1,0:T(8,128)S(1)} %shard_map.37) | data formatting | bytes 131072

commit v2 on v0

--- a/solution.py
+++ b/solution.py
@@ -331,7 +331,7 @@
 
         lax.fori_loop(0, height // inner_rows, inner_chunk, 0)
 
-    for j in range(1, nz):
+    for j in range(1, nz + 1):
         inner_slab(lax.rem(iz + j, nz))
 
     for step in sides:
@@ -358,8 +358,6 @@
 
     for j in range(1, nz + 1):
         slab = lax.rem(iz + j, nz)
-        if j == nz:
-            inner_slab(slab)
 
         at = pl.multiple_of(slab * height, height)
         acc = sample(0, at, height)

time: 22.9 us -> 24.2 us (1.057)
  Pallas kernels: 22.1 us -> 23.5 us
    pallas_call x1, Pallas kernels: 22.1 us -> 23.5 us  [shards(): pl.pallas_call(functools.partial(kernel, sizes, 1.0 / (depth * nz)), out_...]
where the time goes in v2:
time: 24.2 us; the launch traced here: 24.1 us
  Pallas kernels  23.5 us (97%)
  local copies, waits for them, and re-layouts  0.63 us (3%)
    pallas_call x1, Pallas kernels, shards(): pl.pallas_call(functools.partial(kernel, sizes, 1.0 / (depth * nz)), out_...  23.5 us
    unnamed x1, local copies, waits for them, and re-layouts  0.63 us

profile of v2, /device:TPU:0, one launch (start us, length us, event | category | flops | bytes accessed | tf_op | source)
XLA Modules:
  0.0 24.1 jit_solution(17573323212043058331)
XLA Ops:
  0.0 23.5 %shard_map.37 = f32[4,32,128]{2,1,0:T(8,128)S(1)} custom-call(f32[2,16,64,128]{3,2,1,0:T(8,128)} %field.1, f32[4,128]{1,0:T(4,128)} %transfer_in.1, f32[2]{0:T(128)} %angles_in.1), custom_call_target="tpu_custom_call" | custom-call | tf_op jit(solution)/shard_map/pallas_call | solution.py:403
  23.5 0.6 %copy.5 = f32[4,32,128]{2,1,0:T(8,128)} copy(f32[4,32,128]{2,1,0:T(8,128)S(1)} %shard_map.37) | data formatting | bytes 131072
